TPU v7x, 256 devices: a whole 4x4x8 slice. The times are simulated.
256 devices in a mesh: dom: 8 (over z), row: 16 (over y, x), col: 2 (over core).
Axes of the slice: x: 4, y: 4, z: 8, core: 2. Of those that a mesh axis runs over, the one named last changes fastest.
Arguments:
- next_inverse: bfloat16 [8, 4096, 4096], P('dom', 'row', 'col'), may hold values from -6 to 6
- next_arrow: bfloat16 [8, 64, 4096], P('dom', None, 'row'), may hold values from -6 to 6
- factor_win: bfloat16 [8, 4096, 3072], P('dom', 'row', 'col'), may hold values from -0.09375 to 0.09375
- factor_rest: bfloat16 [8, 4096, 1024], P('dom', 'row', 'col'), may hold values from -0.09375 to 0.09375
- arrow_win: bfloat16 [8, 64, 3072], P('dom', None, 'col'), may hold values from -0.75 to 0.75
- arrow_rest: bfloat16 [8, 64, 1024], P('dom', None, 'col'), may hold values from -0.75 to 0.75
- tip_inverse: bfloat16 [64, 64], replicated, may hold values from -6 to 6
- base_win: bfloat16 [8, 3072, 3072], P('dom', 'row', 'col'), may hold values from -6 to 6
- base_rest: bfloat16 [8, 3072, 1024], P('dom', 'row', 'col'), may hold values from -6 to 6
Outputs:
- sub_inverse: bfloat16 [8, 4096, 3072], P('dom', 'row', 'col')
- arrow_inverse: bfloat16 [8, 64, 3072], P('dom', None, 'col')
- diag_win: bfloat16 [8, 3072, 3072], P('dom', 'row', 'col')
- diag_rest: bfloat16 [8, 3072, 1024], P('dom', 'row', 'col')
All inputs are finite; a program needn't handle non-finite values.
Results may differ from a plain program's by a relative error of at most 0.0046.
Values may be sent and summed in bfloat16 or wider, within the bound.
A program may use at most 128 MiB of HBM per device.

v0:
```python
import jax
import jax.numpy as jnp
from jax import lax
from jax.sharding import PartitionSpec as P


def shifted(value, axis, steps):
    count = lax.axis_size(axis)
    leading, last = (max(0, -steps), min(count, count - steps))
    return lax.ppermute(value, axis, [(source, source + steps) for source in range(leading, last)])


def contract_first(left, right):
    return lax.dot_general(
        left, right, (((0,), (0,)), ((), ())), preferred_element_type=jnp.float32
    )


def per_device(
    next_inverse,
    next_arrow,
    factor_win,
    factor_rest,
    arrow_win,
    arrow_rest,
    tip_inverse,
    base_win,
    base_rest,
):
    inverse_tile = next_inverse[0]
    arrow_tile = next_arrow[0]
    factor_tile = factor_win[0]
    factor_other = factor_rest[0]
    ratio_tile = arrow_win[0]
    ratio_other = arrow_rest[0]
    factor_column = lax.all_gather(factor_tile, "row", axis=0, tiled=True)
    inverse_next, arrow_next = shifted((inverse_tile, arrow_tile), "dom", -1)
    start_sum = contract_first(arrow_next, ratio_tile)
    x_total = start_sum + jnp.dot(
        lax.all_gather(inverse_next, "col", axis=1, tiled=True),
        factor_column,
        preferred_element_type=jnp.float32,
    )
    x_bf = x_total.astype(jnp.bfloat16)
    y_part = jnp.dot(arrow_next, factor_tile, preferred_element_type=jnp.float32)
    y_total = lax.psum(y_part, "row") + jnp.dot(
        tip_inverse, ratio_tile, preferred_element_type=jnp.float32
    )
    y_bf = y_total.astype(jnp.bfloat16)
    x_panel, y_panel = (
        lax.all_gather(x_bf, "col", axis=1, tiled=True),
        lax.all_gather(y_bf, "col", axis=1, tiled=True),
    )
    ratio_both = jnp.concatenate([ratio_tile, ratio_other], axis=1)
    rows_here = y_panel.shape[1] // lax.axis_size("row")
    y_rows = lax.dynamic_slice_in_dim(y_panel, lax.axis_index("row") * rows_here, rows_here, 1)
    x_columns = lax.all_to_all(x_panel, "row", split_axis=1, concat_axis=0, tiled=True)
    rest_column = lax.all_gather(factor_other, "row", axis=0, tiled=True)
    factor_full = jnp.concatenate([factor_column, rest_column], axis=1)
    diag_part = contract_first(x_columns, factor_full)
    base_both = jnp.concatenate([base_win[0], base_rest[0]], axis=1).astype(jnp.float32)
    diag_total = base_both + diag_part + contract_first(y_rows, ratio_both)
    split = factor_tile.shape[1]
    diag_left = diag_total[:, :split].astype(jnp.bfloat16)
    diag_right = diag_total[:, split:].astype(jnp.bfloat16)
    return ((-x_bf)[None], (-y_bf)[None], diag_left[None], diag_right[None])


def solution(mesh):
    in_specs = (
        P("dom", "row", "col"),
        P("dom", None, "row"),
        P("dom", "row", "col"),
        P("dom", "row", "col"),
        P("dom", None, "col"),
        P("dom", None, "col"),
        P(),
        P("dom", "row", "col"),
        P("dom", "row", "col"),
    )
    out_specs = (
        P("dom", "row", "col"),
        P("dom", None, "col"),
        P("dom", "row", "col"),
        P("dom", "row", "col"),
    )
    return jax.shard_map(
        per_device, mesh=mesh, in_specs=in_specs, out_specs=out_specs, check_vma=False
    )
```

profile of v0, /device:TPU:1, one launch (start us, length us, event | category | flops | bytes accessed | tf_op | source)
XLA Modules:
  0.0 360.3 jit_solution(10407591954021950761)
XLA Ops:
  7.2 0.0 copy-start
  7.2 0.0 copy-start.7
  7.2 0.0 all-gather.7.cloned.1.call-start
  7.2 1.3 collective-permute-start.1
  8.5 24.2 %collective-permute-done.1 = bf16[256,2048]{1,0:T(8,128)(2,1)S(1)} collective-permute-done((bf16[256,2048]{1,0:T(8,128)(2,1)}, bf16[256,2048]{1,0:T(8,128)(2,1)S(1)}, u32[]{:S(2)}, u32[]{:S(2)}) %collective-permute-start.1) | collective-permute-done | bytes 1048608 | tf_op jit(solution)/shard_map/ppermute | solution.py:10
  32.8 0.0 copy-start.4
  32.8 1.0 copy-done.4
  33.8 0.0 all-gather.7.cloned.1.call-update
  33.8 0.0 all-gather.11.cloned.1.call-start
  33.9 0.7 all-gather.11.cloned.1.call-update
  34.6 0.0 all-gather.9.cloned.1.call-start
  34.6 0.0 copy-done.7
  34.6 0.0 copy-start.3
  34.6 1.4 collective-permute-start
  36.1 19.8 %all-gather.7.cloned.1.call-done = bf16[256,4096]{1,0:T(8,128)(2,1)} async-done(((bf16[256,2048]{1,0:T(8,128)(2,1)}), bf16[256,4096]{1,0:T(8,128)(2,1)}) %all-gather.7.cloned.1.call-update) | async-done | bytes 2097168 | tf_op jit(solution)/shard_map/all_gather | solution.py:40
  55.9 98.0 %all-gather.11.cloned.1.call-done = bf16[1,4096,1536]{2,1,0:T(8,128)(2,1)} async-done(((bf16[1,256,1536]{2,1,0:T(8,128)(2,1)}), bf16[1,4096,1536]{2,1,0:T(8,128)(2,1)}) %all-gather.11.cloned.1.call-update) | async-done | bytes 12582928 | tf_op jit(solution)/shard_map/all_gather | solution.py:36
  153.9 7.0 %fusion.18 = f32[256,1536]{1,0:T(8,128)S(1)} fusion(bf16[256,4096]{1,0:T(8,128)(2,1)} %all-gather.7.cloned.1.call-done, bf16[1,4096,1536]{2,1,0:T(8,128)(2,1)} %all-gather.11.cloned.1.call-done), kind=kOutput, calls=%fused_computation.23 | convolution fusion | flops 3221225472 | bytes 16252928 | tf_op jit(solution)/shard_map/dot_general | solution.py:39
  160.9 0.0 copy-start.2
  160.9 0.0 collective-permute-done
  161.0 0.0 copy-done.3
  161.0 1.3 fusion.4
  162.2 0.0 all-gather.9.cloned.1.call-update
  162.3 0.0 all-reduce.2.cloned.1.call-start
  162.3 0.0 copy-done.2
  162.3 1.0 fusion.9
  163.3 0.0 all-reduce.2.cloned.1.call-update
  163.3 0.0 all-gather.13.cloned.1.call-start
  163.4 0.5 all-gather.13.cloned.1.call-update
  163.9 14.1 %all-gather.9.cloned.1.call-done = bf16[256,3072]{1,0:T(8,128)(2,1)} async-done(((bf16[256,1536]{1,0:T(8,128)(2,1)}), bf16[256,3072]{1,0:T(8,128)(2,1)}) %all-gather.9.cloned.1.call-update) | async-done | bytes 1572880 | tf_op jit(solution)/shard_map/all_gather | solution.py:51
  178.0 2.6 copy.13
  180.6 6.3 %all-to-all-start = ((bf16[256,16,192]{0,2,1:T(8,128)(2,1)}), bf16[256,16,192]{0,2,1:T(8,128)(2,1)S(1)}, u32[]{:S(2)}, u32[]{:S(2)}) async-start(bf16[256,16,192]{0,2,1:T(8,128)(2,1)} %bitcast.9), calls=%async_computation | async-start | bytes 3145728 | tf_op jit(solution)/shard_map/all_to_all | solution.py:57
  186.9 0.0 copy-start.1
  186.9 0.0 copy-done
  186.9 0.2 fusion.20
  187.1 95.9 %all-reduce.2.cloned.1.call-done = f32[64,1536]{1,0:T(8,128)} async-done(((f32[64,1536]{1,0:T(8,128)}), f32[64,1536]{1,0:T(8,128)}) %all-reduce.2.cloned.1.call-update) | async-done | bytes 393232 | tf_op jit(solution)/shard_map/psum | solution.py:46
  283.0 1.7 negate_bitcast_fusion.1
  284.7 3.8 %all_gather.19 = bf16[64,3072]{1,0:T(8,128)(2,1)} all-gather(bf16[64,1536]{1,0:T(8,128)(2,1)S(1)} %get-tuple-element.5), channel_id=1, replica_groups=mesh['dom'=8,'row'=16,'col'=2] {'col'}, dimensions={1}, use_global_device_ids=true | all-gather | bytes 589824 | tf_op jit(solution)/shard_map/all_gather | solution.py:52
  288.5 0.0 copy-done.1
  288.5 0.9 negate_bitcast_fusion
  289.4 0.0 all-to-all-done
  289.4 0.2 copy.15
  289.6 53.0 %all-gather.13.cloned.1.call-done = bf16[1,4096,512]{2,1,0:T(8,128)(2,1)} async-done(((bf16[1,256,512]{2,1,0:T(8,128)(2,1)}), bf16[1,4096,512]{2,1,0:T(8,128)(2,1)}) %all-gather.13.cloned.1.call-update) | async-done | bytes 4194320 | tf_op jit(solution)/shard_map/all_gather | solution.py:58
  342.6 0.0 copy-done.6
  342.6 8.4 %fusion.5 = f32[192,2048]{1,0:T(8,128)S(1)} fusion(bf16[4096,192]{0,1:T(8,128)(2,1)S(1)} %bitcast.36, bf16[4096,512]{1,0:T(8,128)(2,1)} %bitcast.39, bf16[4096,1536]{1,0:T(8,128)(2,1)} %bitcast.38, bf16[192,512]{1,0:T(8,128)(2,1)S(1)} %bitcast.42, bf16[192,1536]{1,0:T(8,128)(2,1)} %bitcast.41), kind=kOutput, calls=%fused_computation.7 | convolution fusion | flops 3256745984 | bytes 20709376 | tf_op jit(solution)/shard_map/dot_general | solution.py:14
  350.9 0.0 copy-done.5
  351.0 1.3 fusion.8
  352.2 0.9 slice_bitcast_fusion
  353.1 0.7 slice_bitcast_fusion.1
  (2 shorter events, 0.0 us)
Async XLA Ops:
  7.2 179.7 %copy-start = (bf16[64,64]{1,0:T(8,128)(2,1)S(1)}, bf16[64,64]{1,0:T(8,128)(2,1)}, u32[]{:S(2)}) copy-start(bf16[64,64]{1,0:T(8,128)(2,1)} %param.15) | copy-start | bytes 24580
  7.2 27.4 %copy-start.7 = (bf16[1,64,256]{2,1,0:T(8,128)(2,1)S(1)}, bf16[1,64,256]{2,1,0:T(8,128)(2,1)}, u32[]{:S(2)}) copy-start(bf16[1,64,256]{2,1,0:T(8,128)(2,1)} %param.10) | copy-start | bytes 98308
  7.2 48.7 %all-gather.7.cloned.1.call-start = ((), (), s32[]{:S(2)}) async-start(), calls=%async_computation.1 | async-start | bytes 3145728 | tf_op jit(solution)/shard_map/all_gather | solution.py:40
  7.2 25.5 %collective-permute-start.1 = (bf16[256,2048]{1,0:T(8,128)(2,1)}, bf16[256,2048]{1,0:T(8,128)(2,1)S(1)}, u32[]{:S(2)}, u32[]{:S(2)}) collective-permute-start(bf16[256,2048]{1,0:T(8,128)(2,1)} %bitcast.40), channel_id=1, source_target_pairs={{32,0},{64,32},{96,64},{128,96},{160,128},{192,160},{224,192},{33,... | collective-permute-start | bytes 3145736 | tf_op jit(solution)/shard_map/ppermute | solution.py:10
  32.8 1.0 copy-start.4
  33.8 120.1 %all-gather.11.cloned.1.call-start = ((), (), s32[]{:S(2)}) async-start(), calls=%async_computation.4 | async-start | bytes 13369344 | tf_op jit(solution)/shard_map/all_gather | solution.py:36
  34.6 143.5 %all-gather.9.cloned.1.call-start = ((), (), s32[]{:S(2)}) async-start(), calls=%async_computation.3 | async-start | bytes 2359296 | tf_op jit(solution)/shard_map/all_gather | solution.py:51
  34.6 126.3 %copy-start.3 = (bf16[1,64,1536]{2,1,0:T(8,128)(2,1)S(1)}, bf16[1,64,1536]{2,1,0:T(8,128)(2,1)}, u32[]{:S(2)}) copy-start(bf16[1,64,1536]{2,1,0:T(8,128)(2,1)} %param.13) | copy-start | bytes 589828
  34.6 126.3 %collective-permute-start = (bf16[64,256]{1,0:T(8,128)(2,1)S(1)}, bf16[64,256]{1,0:T(8,128)(2,1)S(1)}, u32[]{:S(2)}, u32[]{:S(2)}) collective-permute-start(bf16[64,256]{1,0:T(8,128)(2,1)S(1)} %bitcast.43), channel_id=1, source_target_pairs={{32,0},{64,32},{96,64},{128,96},{160,128},{192,160},{224,192},{33,... | collective-permute-start | bytes 98312 | tf_op jit(solution)/shard_map/ppermute | solution.py:10
  160.9 1.4 copy-start.2
  162.3 120.7 %all-reduce.2.cloned.1.call-start = ((), (), s32[]{:S(2)}) async-start(), calls=%async_computation.2 | async-start | bytes 786432 | tf_op jit(solution)/shard_map/psum | solution.py:46
  163.3 179.2 %all-gather.13.cloned.1.call-start = ((), (), s32[]{:S(2)}) async-start(), calls=%async_computation.5 | async-start | bytes 4456448 | tf_op jit(solution)/shard_map/all_gather | solution.py:58
  180.6 108.8 %all-to-all-start = ((bf16[256,16,192]{0,2,1:T(8,128)(2,1)}), bf16[256,16,192]{0,2,1:T(8,128)(2,1)S(1)}, u32[]{:S(2)}, u32[]{:S(2)}) async-start(bf16[256,16,192]{0,2,1:T(8,128)(2,1)} %bitcast.9), calls=%async_computation | async-start | bytes 3145728 | tf_op jit(solution)/shard_map/all_to_all | solution.py:57
  186.9 101.6 %copy-start.1 = (bf16[256,1536]{1,0:T(8,128)(2,1)S(1)}, bf16[256,1536]{1,0:T(8,128)(2,1)}, u32[]{:S(2)}) copy-start(bf16[256,1536]{1,0:T(8,128)(2,1)} %fusion.4) | copy-start | bytes 2359300
  289.4 53.1 %copy-start.6 = (bf16[1,192,512]{2,1,0:T(8,128)(2,1)S(1)}, bf16[1,192,512]{2,1,0:T(8,128)(2,1)}, u32[]{:S(2)}) copy-start(bf16[1,192,512]{2,1,0:T(8,128)(2,1)} %param.17) | copy-start | bytes 589828
  342.6 8.4 %copy-start.5 = (bf16[1,64,512]{2,1,0:T(8,128)(2,1)S(1)}, bf16[1,64,512]{2,1,0:T(8,128)(2,1)}, u32[]{:S(2)}) copy-start(bf16[1,64,512]{2,1,0:T(8,128)(2,1)} %param.14) | copy-start | bytes 196612
Sparse Core Ops, SparseCore 0:
  33.9 21.8 all-gather.6
  58.3 95.5 all-gather.10
  162.4 15.6 all-gather.8
  181.7 101.2 all-reduce.1
  285.3 57.2 all-gather.12
where the time goes:
time: 361 us; the launch traced here: 360 us
  waiting for transfers between devices  306 us (85%)
  matrix products  19.1 us (5%)
  between operations  13.9 us (4%)
  starting transfers between devices  9.18 us (3%)
  local copies, waits for them, and re-layouts  5.35 us (1%)
  blocking collectives  3.8 us (1%)
    all_gather x1, waiting for transfers between devices, per_device(): factor_column = lax.all_gather(factor_tile, 'row', axis=0, tiled=True)  98 us
    psum x1, waiting for transfers between devices, per_device(): lax.psum(y_part, 'row')  95.9 us
    all_gather x1, waiting for transfers between devices, per_device(): rest_column = lax.all_gather(factor_other, 'row', axis=0, tiled=True)  53 us
    ppermute x2, waiting for transfers between devices, shifted(): lax.ppermute(value, axis, [(source, source + steps) for source in range(l...  24.2 us
    all_gather x1, waiting for transfers between devices, per_device(): lax.all_gather(inverse_next, 'col', axis=1, tiled=True)  19.8 us
    all_gather x1, waiting for transfers between devices, per_device(): lax.all_gather(x_bf, 'col', axis=1, tiled=True)  14.1 us
    dot_general x3, matrix products, contract_first(): lax.dot_general(left, right, (((0,), (0,)), ((), ())), preferred_element_...  10.9 us
  transfers between devices with their start and end apart: 8, of which 6 were waited for; matrix products, arithmetic and copies ran while one was open for 4% of the time, Pallas kernels for 0%

commit v1 on v0

--- a/solution.py
+++ b/solution.py
@@ -37,7 +37,9 @@
     inverse_next, arrow_next = shifted((inverse_tile, arrow_tile), "dom", -1)
     start_sum = contract_first(arrow_next, ratio_tile)
     x_total = start_sum + jnp.dot(
-        lax.all_gather(inverse_next, "col", axis=1, tiled=True),
+        jnp.concatenate(
+            lax.all_to_all(jnp.stack([inverse_next] * lax.axis_size("col")), "col", 0, 0), axis=1
+        ),
         factor_column,
         preferred_element_type=jnp.float32,
     )

time: 361 us -> 316 us (0.88)
  waiting for transfers between devices: 306 us -> 253 us
  blocking collectives: 3.8 us -> 12.2 us
    all_gather x1, waiting for transfers between devices: 98 us -> 65.8 us  [per_device(): factor_column = lax.all_gather(factor_tile, 'row', axis=0, tiled=True)]
    all_gather x1 -> x0, waiting for transfers between devices: 19.8 us -> none  [per_device(): lax.all_gather(inverse_next, 'col', axis=1, tiled=True)]
    all_to_all x0 -> x1, blocking collectives: none -> 8.44 us  [per_device(): lax.all_to_all(jnp.stack([inverse_next] * lax.axis_size('col')), 'col', 0...]
  transfers between devices with their start and end apart: 8 -> 7, of which waited for: 6 -> 5; matrix products, arithmetic and copies ran while one was open for 4% -> 5% of each run, Pallas kernels for 0% -> 0%
where the time goes in v1:
time: 316 us; the launch traced here: 315 us
  waiting for transfers between devices  253 us (80%)
  matrix products  18.6 us (6%)
  between operations  13.9 us (4%)
  blocking collectives  12.2 us (4%)
  starting transfers between devices  9.14 us (3%)
  local copies, waits for them, and re-layouts  5.82 us (2%)
    psum x1, waiting for transfers between devices, per_device(): lax.psum(y_part, 'row')  95.9 us
    all_gather x1, waiting for transfers between devices, per_device(): factor_column = lax.all_gather(factor_tile, 'row', axis=0, tiled=True)  65.8 us
    all_gather x1, waiting for transfers between devices, per_device(): rest_column = lax.all_gather(factor_other, 'row', axis=0, tiled=True)  53 us
    ppermute x2, waiting for transfers between devices, shifted(): lax.ppermute(value, axis, [(source, source + steps) for source in range(l...  22.8 us
    all_gather x1, waiting for transfers between devices, per_device(): lax.all_gather(x_bf, 'col', axis=1, tiled=True)  14.1 us
    dot_general x3, matrix products, contract_first(): lax.dot_general(left, right, (((0,), (0,)), ((), ())), preferred_element_...  10.9 us
    all_to_all x1, blocking collectives, per_device(): lax.all_to_all(jnp.stack([inverse_next] * lax.axis_size('col')), 'col', 0...  8.44 us
    dot_general x1, matrix products, per_device(): jnp.dot(jnp.concatenate(lax.all_to_all(jnp.stack([inverse_next] * lax.axi...  6.49 us
  transfers between devices with their start and end apart: 7, of which 5 were waited for; matrix products, arithmetic and copies ran while one was open for 5% of the time, Pallas kernels for 0%

profile of v1, /device:TPU:1, one launch (start us, length us, event | category | flops | bytes accessed | tf_op | source)
XLA Modules:
  0.0 315.3 jit_solution(12135798471707156134)
XLA Ops:
  7.2 0.0 copy-start
  7.2 0.0 copy-start.6
  7.2 0.0 all-gather.8.cloned.1.call-start
  7.2 0.7 all-gather.8.cloned.1.call-update
  7.9 0.0 all-gather.6.cloned.1.call-start
  8.0 1.5 copy.13
  9.5 1.3 collective-permute-start.1
  10.8 0.0 copy-done.6
  10.8 1.3 collective-permute-start
  12.1 22.8 %collective-permute-done.1 = bf16[256,2048]{0,1:T(8,128)(2,1)S(1)} collective-permute-done((bf16[256,2048]{0,1:T(8,128)(2,1)S(1)}, bf16[256,2048]{0,1:T(8,128)(2,1)S(1)}, u32[]{:S(2)}, u32[]{:S(2)}) %collective-permute-start.1) | collective-permute-done | bytes 1048608 | tf_op jit(solution)/shard_map/ppermute | solution.py:10
  34.9 0.2 pad_maximum_fusion
  35.1 8.4 %all_to_all.24 = bf16[2,256,2048]{1,2,0:T(8,128)(2,1)S(1)} all-to-all(bf16[2,256,2048]{1,2,0:T(8,128)(2,1)S(1)} %pad_maximum_fusion), channel_id=1, replica_groups=mesh['dom'=8,'row'=16,'col'=2] {'col'}, dimensions={0} | all-to-all | bytes 4194304 | tf_op jit(solution)/shard_map/all_to_all | solution.py:41
  43.5 65.8 %all-gather.8.cloned.1.call-done = bf16[1,4096,1536]{2,1,0:T(8,128)(2,1)} async-done(((bf16[1,256,1536]{2,1,0:T(8,128)(2,1)}), bf16[1,4096,1536]{2,1,0:T(8,128)(2,1)}) %all-gather.8.cloned.1.call-update) | async-done | bytes 12582928 | tf_op jit(solution)/shard_map/all_gather | solution.py:36
  109.3 0.0 copy-start.3
  109.3 6.5 %fusion.18 = f32[256,1536]{1,0:T(8,128)S(1)} fusion(bf16[256,4096]{0,1:T(8,128)(2,1)S(1)} %bitcast.39, bf16[1,4096,1536]{2,1,0:T(8,128)(2,1)} %all-gather.8.cloned.1.call-done), kind=kOutput, calls=%fused_computation.24 | convolution fusion | flops 3221225472 | bytes 16252928 | tf_op jit(solution)/shard_map/dot_general | solution.py:39
  115.8 0.0 copy-start.2
  115.8 0.0 collective-permute-done
  115.8 0.0 copy-done.3
  115.8 1.3 fusion.4
  117.1 0.0 all-gather.6.cloned.1.call-update
  117.1 0.0 all-reduce.2.cloned.1.call-start
  117.2 0.0 copy-done.2
  117.2 1.0 fusion.9
  118.2 0.0 all-reduce.2.cloned.1.call-update
  118.2 0.0 all-gather.10.cloned.1.call-start
  118.3 0.5 all-gather.10.cloned.1.call-update
  118.8 14.1 %all-gather.6.cloned.1.call-done = bf16[256,3072]{1,0:T(8,128)(2,1)} async-done(((bf16[256,1536]{1,0:T(8,128)(2,1)}), bf16[256,3072]{1,0:T(8,128)(2,1)}) %all-gather.6.cloned.1.call-update) | async-done | bytes 1572880 | tf_op jit(solution)/shard_map/all_gather | solution.py:53
  132.9 2.6 copy.14
  135.5 0.0 copy-start.1
  135.5 6.4 %all-to-all-start.1 = ((bf16[256,16,192]{0,2,1:T(8,128)(2,1)}), bf16[256,16,192]{0,2,1:T(8,128)(2,1)S(1)}, u32[]{:S(2)}, u32[]{:S(2)}) async-start(bf16[256,16,192]{0,2,1:T(8,128)(2,1)} %bitcast.41), calls=%async_computation.1 | async-start | bytes 3145728 | tf_op jit(solution)/shard_map/all_to_all | solution.py:59
  141.9 0.0 copy-done
  141.9 0.2 fusion.20
  142.1 95.9 %all-reduce.2.cloned.1.call-done = f32[64,1536]{1,0:T(8,128)} async-done(((f32[64,1536]{1,0:T(8,128)}), f32[64,1536]{1,0:T(8,128)}) %all-reduce.2.cloned.1.call-update) | async-done | bytes 393232 | tf_op jit(solution)/shard_map/psum | solution.py:48
  238.0 1.7 negate_bitcast_fusion.1
  239.7 3.8 %all_gather.15 = bf16[64,3072]{1,0:T(8,128)(2,1)} all-gather(bf16[64,1536]{1,0:T(8,128)(2,1)S(1)} %get-tuple-element.5), channel_id=1, replica_groups=mesh['dom'=8,'row'=16,'col'=2] {'col'}, dimensions={1}, use_global_device_ids=true | all-gather | bytes 589824 | tf_op jit(solution)/shard_map/all_gather | solution.py:54
  243.5 0.0 copy-done.1
  243.5 0.0 copy-start.5
  243.5 0.9 negate_bitcast_fusion
  244.4 0.0 all-to-all-done.1
  244.4 0.2 copy.16
  244.6 53.0 %all-gather.10.cloned.1.call-done = bf16[1,4096,512]{2,1,0:T(8,128)(2,1)} async-done(((bf16[1,256,512]{2,1,0:T(8,128)(2,1)}), bf16[1,4096,512]{2,1,0:T(8,128)(2,1)}) %all-gather.10.cloned.1.call-update) | async-done | bytes 4194320 | tf_op jit(solution)/shard_map/all_gather | solution.py:60
  297.6 0.0 copy-done.5
  297.6 0.0 copy-start.4
  297.6 8.4 %fusion.5 = f32[192,2048]{1,0:T(8,128)S(1)} fusion(bf16[4096,192]{0,1:T(8,128)(2,1)S(1)} %bitcast.43, bf16[4096,512]{1,0:T(8,128)(2,1)} %bitcast.47, bf16[4096,1536]{1,0:T(8,128)(2,1)} %bitcast.38, bf16[192,512]{1,0:T(8,128)(2,1)S(1)} %bitcast.49, bf16[192,1536]{1,0:T(8,128)(2,1)} %bitcast.48), kind=kOutput, calls=%fused_computation.7 | convolution fusion | flops 3256745984 | bytes 20709376 | tf_op jit(solution)/shard_map/dot_general | solution.py:14
  305.9 0.0 copy-done.4
  306.0 1.3 fusion.8
  307.2 0.9 slice_bitcast_fusion
  308.1 0.7 slice_bitcast_fusion.1
Async XLA Ops:
  7.2 134.7 %copy-start = (bf16[64,64]{1,0:T(8,128)(2,1)S(1)}, bf16[64,64]{1,0:T(8,128)(2,1)}, u32[]{:S(2)}) copy-start(bf16[64,64]{1,0:T(8,128)(2,1)} %param.15) | copy-start | bytes 24580
  7.2 3.6 %copy-start.6 = (bf16[1,64,256]{2,1,0:T(8,128)(2,1)S(1)}, bf16[1,64,256]{2,1,0:T(8,128)(2,1)}, u32[]{:S(2)}) copy-start(bf16[1,64,256]{2,1,0:T(8,128)(2,1)} %param.10) | copy-start | bytes 98308
  7.2 102.1 %all-gather.8.cloned.1.call-start = ((), (), s32[]{:S(2)}) async-start(), calls=%async_computation.4 | async-start | bytes 13369344 | tf_op jit(solution)/shard_map/all_gather | solution.py:36
  7.9 125.0 %all-gather.6.cloned.1.call-start = ((), (), s32[]{:S(2)}) async-start(), calls=%async_computation.3 | async-start | bytes 2359296 | tf_op jit(solution)/shard_map/all_gather | solution.py:53
  9.5 25.4 %collective-permute-start.1 = (bf16[256,2048]{0,1:T(8,128)(2,1)S(1)}, bf16[256,2048]{0,1:T(8,128)(2,1)S(1)}, u32[]{:S(2)}, u32[]{:S(2)}) collective-permute-start(bf16[256,2048]{0,1:T(8,128)(2,1)S(1)} %bitcast.45), channel_id=1, source_target_pairs={{32,0},{64,32},{96,64},{128,96},{160,128},{192,160},{224,192},{33,... | collective-permute-start | bytes 3145736 | tf_op jit(solution)/shard_map/ppermute | solution.py:10
  10.8 105.1 %collective-permute-start = (bf16[64,256]{1,0:T(8,128)(2,1)S(1)}, bf16[64,256]{1,0:T(8,128)(2,1)S(1)}, u32[]{:S(2)}, u32[]{:S(2)}) collective-permute-start(bf16[64,256]{1,0:T(8,128)(2,1)S(1)} %bitcast.50), channel_id=1, source_target_pairs={{32,0},{64,32},{96,64},{128,96},{160,128},{192,160},{224,192},{33,... | collective-permute-start | bytes 98312 | tf_op jit(solution)/shard_map/ppermute | solution.py:10
  109.3 6.5 %copy-start.3 = (bf16[1,64,1536]{2,1,0:T(8,128)(2,1)S(1)}, bf16[1,64,1536]{2,1,0:T(8,128)(2,1)}, u32[]{:S(2)}) copy-start(bf16[1,64,1536]{2,1,0:T(8,128)(2,1)} %param.13) | copy-start | bytes 589828
  115.8 1.4 copy-start.2
  117.1 120.8 %all-reduce.2.cloned.1.call-start = ((), (), s32[]{:S(2)}) async-start(), calls=%async_computation.2 | async-start | bytes 786432 | tf_op jit(solution)/shard_map/psum | solution.py:48
  118.2 179.3 %all-gather.10.cloned.1.call-start = ((), (), s32[]{:S(2)}) async-start(), calls=%async_computation.5 | async-start | bytes 4456448 | tf_op jit(solution)/shard_map/all_gather | solution.py:60
  135.5 108.0 %copy-start.1 = (bf16[256,1536]{1,0:T(8,128)(2,1)S(1)}, bf16[256,1536]{1,0:T(8,128)(2,1)}, u32[]{:S(2)}) copy-start(bf16[256,1536]{1,0:T(8,128)(2,1)} %fusion.4) | copy-start | bytes 2359300
  135.5 108.9 %all-to-all-start.1 = ((bf16[256,16,192]{0,2,1:T(8,128)(2,1)}), bf16[256,16,192]{0,2,1:T(8,128)(2,1)S(1)}, u32[]{:S(2)}, u32[]{:S(2)}) async-start(bf16[256,16,192]{0,2,1:T(8,128)(2,1)} %bitcast.41), calls=%async_computation.1 | async-start | bytes 3145728 | tf_op jit(solution)/shard_map/all_to_all | solution.py:59
  243.5 54.1 %copy-start.5 = (bf16[1,192,512]{2,1,0:T(8,128)(2,1)S(1)}, bf16[1,192,512]{2,1,0:T(8,128)(2,1)}, u32[]{:S(2)}) copy-start(bf16[1,192,512]{2,1,0:T(8,128)(2,1)} %param.17) | copy-start | bytes 589828
  297.6 8.4 %copy-start.4 = (bf16[1,64,512]{2,1,0:T(8,128)(2,1)S(1)}, bf16[1,64,512]{2,1,0:T(8,128)(2,1)}, u32[]{:S(2)}) copy-start(bf16[1,64,512]{2,1,0:T(8,128)(2,1)} %param.14) | copy-start | bytes 196612
Sparse Core Ops, SparseCore 0:
  10.5 98.8 all-gather.7
  117.3 15.5 all-gather.5
  136.7 101.2 all-reduce.1
  240.3 57.2 all-gather.9
